TPU v7x, 32 devices: a whole 2x2x4 slice. The times are simulated.
32 devices in a mesh: dp: 8 (over y, x, core), tensor: 4 (over z).
Axes of the slice: x: 2, y: 2, z: 4, core: 2. Of those that a mesh axis runs over, the one named last changes fastest.
Arguments:
- activations: bfloat16 [584, 16, 1024], P('tensor', 'dp'), may hold values from -6 to 6
- cotangent: bfloat16 [584, 16, 1024], P('tensor', 'dp'), may hold values from -6 to 6
- token_valid: int32 [16, 584], P('dp'), may hold values from 0 to 1, as said below
- image_counts: int32 [8], P('dp'), may hold values from 1 to 2, as said below
- pre_gain: bfloat16 [1024], P('dp'), may hold values from 0.5 to 1.5
- pre_shift: bfloat16 [1024], P('dp'), may hold values from -3 to 3
- attn_weight: bfloat16 [3, 1024, 1024], P(None, 'dp', 'tensor'), may hold values from -0.1875 to 0.1875
- attn_bias: bfloat16 [2, 1024], P(None, 'tensor'), may hold values from -3 to 3
- proj_weight: bfloat16 [1024, 1024], P('tensor', 'dp'), may hold values from -0.5 to 0.5
- proj_bias: bfloat16 [1024], P('dp'), may hold values from -3 to 3
- mid_gain: bfloat16 [1024], P('dp'), may hold values from 0.5 to 1.5
- mid_shift: bfloat16 [1024], P('dp'), may hold values from -3 to 3
- up_weight: bfloat16 [1024, 4096], P('dp', 'tensor'), may hold values from -0.1875 to 0.1875
- up_bias: bfloat16 [4096], P('tensor'), may hold values from -3 to 3
- down_weight: bfloat16 [4096, 1024], P('tensor', 'dp'), may hold values from -0.09375 to 0.09375
- down_bias: bfloat16 [1024], P('dp'), may hold values from -3 to 3
Outputs:
- block_out: bfloat16 [584, 16, 1024], P('tensor', 'dp')
- input_grad: float32 [584, 16, 1024], P('tensor', 'dp')
- pregain_grad: float32 [1024], P('dp')
- preshift_grad: float32 [1024], P('dp')
- attnweight_grad: float32 [3, 1024, 1024], P(None, 'dp', 'tensor')
- attnbias_grad: float32 [2, 1024], P(None, 'tensor')
- projweight_grad: float32 [1024, 1024], P('tensor', 'dp')
- projbias_grad: float32 [1024], P('dp')
- midgain_grad: float32 [1024], P('dp')
- midshift_grad: float32 [1024], P('dp')
- upweight_grad: float32 [1024, 4096], P('dp', 'tensor')
- upbias_grad: float32 [4096], P('tensor')
- downweight_grad: float32 [4096, 1024], P('tensor', 'dp')
- downbias_grad: float32 [1024], P('dp')
Inputs may be any that keep to these rules, and one draw needn't show every extreme that they name: `token_valid`: the valid tokens of each image are a leading run of 292 or more positions, followed only by padding. The slots of a dp index that hold images are its first image_counts ones; in every draw some dp index holds 2 images.
All inputs are finite; a program needn't handle non-finite values.
Results may differ from a plain program's by a relative error of at most 0.012.
Values may be sent and summed in bfloat16 or wider, within the bound.
A program may use at most 192 MiB of HBM per device.

v0:
```python
import jax
import jax.numpy as jnp
from jax import lax
from jax.sharding import PartitionSpec as P

D = 1024
H = 16
HD = 64
MB = 2
EPS = 1e-06
NEG = -1000000000.0


def layer_norm(values, gain, shift):
    center = values - jnp.mean(values, axis=-1, keepdims=True)
    spread = jnp.mean(center * center, axis=-1, keepdims=True)
    return center * lax.rsqrt(spread + EPS) * gain + shift


def gelu_exact(values):
    return jax.nn.gelu(values, approximate=False)


def per_device(
    activations,
    cotangent,
    token_valid,
    image_counts,
    pre_gain,
    pre_shift,
    attn_weight,
    attn_bias,
    proj_weight,
    proj_bias,
    mid_gain,
    mid_shift,
    up_weight,
    up_bias,
    down_weight,
    down_bias,
):
    f32 = jnp.float32
    bf16 = jnp.bfloat16
    tensor_size = lax.axis_size("tensor")
    local_rows = activations.shape[0]
    slots = activations.shape[1]
    per_micro = slots // MB
    heads_here = H // tensor_size
    width_here = attn_weight.shape[2]
    hidden_here = up_weight.shape[1]
    scale = HD ** (-0.5)
    first_row = lax.axis_index("tensor") * local_rows
    my_valid = lax.dynamic_slice_in_dim(token_valid, first_row, local_rows, 1).astype(f32)
    slot_live = (jnp.arange(slots, dtype=jnp.int32) < image_counts[0]).astype(f32)
    attn_bias_f = attn_bias.astype(f32)
    up_bias_f = up_bias.astype(f32)
    acc_attn = jnp.zeros((3, D, width_here), f32)
    acc_proj = jnp.zeros((width_here, D), f32)
    acc_up = jnp.zeros((D, hidden_here), f32)
    acc_down = jnp.zeros((hidden_here, D), f32)
    acc_attn_bias = jnp.zeros((2, width_here), f32)
    acc_up_bias = jnp.zeros((hidden_here,), f32)
    acc_vectors = [jnp.zeros((D,), f32) for unused in range(6)]
    block_parts = []
    input_parts = []
    for micro_step in range(MB):
        gathered = (
            lax.all_gather(attn_weight, "dp", axis=1, tiled=True),
            lax.all_gather(proj_weight, "dp", axis=1, tiled=True),
            lax.all_gather(up_weight, "dp", axis=0, tiled=True),
            lax.all_gather(down_weight, "dp", axis=1, tiled=True),
            lax.all_gather(pre_gain, "dp", axis=0, tiled=True),
            lax.all_gather(pre_shift, "dp", axis=0, tiled=True),
            lax.all_gather(proj_bias, "dp", axis=0, tiled=True),
            lax.all_gather(mid_gain, "dp", axis=0, tiled=True),
            lax.all_gather(mid_shift, "dp", axis=0, tiled=True),
            lax.all_gather(down_bias, "dp", axis=0, tiled=True),
        )
        qkv_full, proj_full, upw_full, downw_full = (
            gathered[0],
            gathered[1],
            gathered[2],
            gathered[3],
        )
        gain_one, shift_one, proj_bias_f, gain_two, shift_two, down_bias_f = [
            item.astype(f32) for item in gathered[4:]
        ]
        offset = micro_step * per_micro
        inputs_f = activations[:, offset : offset + per_micro].astype(f32)
        key_valid = token_valid[offset : offset + per_micro]
        key_bias = jnp.where(key_valid > 0, 0.0, NEG).astype(f32)
        out_mask = jnp.transpose(
            slot_live[offset : offset + per_micro][:, None] * my_valid[offset : offset + per_micro]
        )[:, :, None]
        normed = layer_norm(inputs_f, gain_one, shift_one).astype(bf16)
        normed_all = lax.all_gather(normed, "tensor", axis=0, tiled=True)
        full_rows = normed_all.shape[0]
        projected = jnp.einsum("sid,cde->csie", normed_all, qkv_full, preferred_element_type=f32)
        queries = (
            (projected[0] + attn_bias_f[0])
            .astype(bf16)
            .reshape(full_rows, per_micro, heads_here, HD)
        )
        keys = projected[1].astype(bf16).reshape(full_rows, per_micro, heads_here, HD)
        values = (
            (projected[2] + attn_bias_f[1])
            .astype(bf16)
            .reshape(full_rows, per_micro, heads_here, HD)
        )

        def scores_of(query_part, key_part):
            raw = jnp.einsum("qihe,kihe->ihqk", query_part, key_part, preferred_element_type=f32)
            return raw * scale + key_bias[:, None, None, :]

        scores = scores_of(queries, keys)
        top = jnp.max(scores, axis=-1, keepdims=True)
        expo = jnp.exp(scores - top)
        total = jnp.sum(expo, axis=-1, keepdims=True)
        logsum = top + jnp.log(total)
        probs_low = (expo / total).astype(bf16)
        attended = (
            jnp.einsum("ihqk,kihe->qihe", probs_low, values, preferred_element_type=f32)
            .astype(bf16)
            .reshape(full_rows, per_micro, width_here)
        )
        resid = (
            inputs_f
            + lax.psum_scatter(
                jnp.einsum("sie,ed->sid", attended, proj_full, preferred_element_type=f32),
                "tensor",
                scatter_dimension=0,
                tiled=True,
            )
            + proj_bias_f
        )
        normed2 = layer_norm(resid, gain_two, shift_two).astype(bf16)
        normed2_all = lax.all_gather(normed2, "tensor", axis=0, tiled=True)
        hidden_pre = (
            jnp.einsum("sid,df->sif", normed2_all, upw_full, preferred_element_type=f32) + up_bias_f
        )
        hidden = gelu_exact(hidden_pre).astype(bf16)
        mlp_out = (
            lax.psum_scatter(
                jnp.einsum("sif,fd->sid", hidden, downw_full, preferred_element_type=f32).astype(
                    jnp.bfloat16
                ),
                "tensor",
                scatter_dimension=0,
                tiled=True,
            ).astype(jnp.float32)
            + down_bias_f
        )
        block_parts.append(((resid + mlp_out) * out_mask).astype(bf16))
        outer = cotangent[:, offset : offset + per_micro].astype(f32) * out_mask
        mlp_grad = outer.astype(bf16)
        acc_vectors[5] = acc_vectors[5] + jnp.sum(mlp_grad.astype(f32), axis=(0, 1))
        mlp_grad_all = lax.all_gather(mlp_grad, "tensor", axis=0, tiled=True)
        acc_down = acc_down + jnp.einsum(
            "sif,sid->fd", hidden, mlp_grad_all, preferred_element_type=f32
        )
        hidden_grad = jnp.einsum(
            "sid,fd->sif", mlp_grad_all, downw_full, preferred_element_type=f32
        )
        unused, gelu_back = jax.vjp(gelu_exact, hidden_pre)
        pre_grad = gelu_back(hidden_grad)[0].astype(bf16)
        acc_up_bias = acc_up_bias + jnp.sum(pre_grad.astype(f32), axis=(0, 1))
        acc_up = acc_up + jnp.einsum(
            "sid,sif->df", normed2_all, pre_grad, preferred_element_type=f32
        )
        normed2_grad = lax.psum_scatter(
            jnp.einsum("sif,df->sid", pre_grad, upw_full, preferred_element_type=f32),
            "tensor",
            scatter_dimension=0,
            tiled=True,
        )
        unused, second_back = jax.vjp(layer_norm, resid, gain_two, shift_two)
        resid_part, gain_two_grad, shift_two_grad = second_back(normed2_grad)
        acc_vectors[3] = acc_vectors[3] + gain_two_grad
        acc_vectors[4] = acc_vectors[4] + shift_two_grad
        resid_grad = outer + resid_part
        branch_grad = resid_grad.astype(bf16)
        acc_vectors[2] = acc_vectors[2] + jnp.sum(branch_grad.astype(f32), axis=(0, 1))
        branch_all = lax.all_gather(branch_grad, "tensor", axis=0, tiled=True)
        acc_proj = acc_proj + jnp.einsum(
            "sie,sid->ed", attended, branch_all, preferred_element_type=f32
        )
        att_grad = (
            jnp.einsum("sid,ed->sie", branch_all, proj_full, preferred_element_type=f32)
            .astype(bf16)
            .reshape(full_rows, per_micro, heads_here, HD)
        )
        probs = jnp.exp(scores_of(queries, keys) - logsum)
        probs_again = probs.astype(bf16)
        value_grad = jnp.einsum(
            "ihqk,qihe->kihe", probs_again, att_grad, preferred_element_type=f32
        ).astype(bf16)
        prob_grad = jnp.einsum("qihe,kihe->ihqk", att_grad, values, preferred_element_type=f32)
        score_grad = (
            probs * (prob_grad - jnp.sum(prob_grad * probs, axis=-1, keepdims=True))
        ).astype(bf16)
        query_grad = (
            jnp.einsum("ihqk,kihe->qihe", score_grad, keys, preferred_element_type=f32) * scale
        ).astype(bf16)
        key_grad = (
            jnp.einsum("ihqk,qihe->kihe", score_grad, queries, preferred_element_type=f32) * scale
        ).astype(bf16)
        qkv_grad = jnp.stack([query_grad, key_grad, value_grad]).reshape(
            3, full_rows, per_micro, width_here
        )
        acc_attn_bias = acc_attn_bias + jnp.stack(
            [
                jnp.sum(qkv_grad[0].astype(f32), axis=(0, 1)),
                jnp.sum(qkv_grad[2].astype(f32), axis=(0, 1)),
            ]
        )
        acc_attn = acc_attn + jnp.einsum(
            "sid,csie->cde", normed_all, qkv_grad, preferred_element_type=f32
        )
        normed_grad = lax.psum_scatter(
            jnp.einsum("csie,cde->sid", qkv_grad, qkv_full, preferred_element_type=f32),
            "tensor",
            scatter_dimension=0,
            tiled=True,
        )
        unused, first_back = jax.vjp(layer_norm, inputs_f, gain_one, shift_one)
        input_part, gain_one_grad, shift_one_grad = first_back(normed_grad)
        acc_vectors[0] = acc_vectors[0] + gain_one_grad
        acc_vectors[1] = acc_vectors[1] + shift_one_grad
        input_parts.append(resid_grad + input_part)
    summed = lax.psum(
        (
            acc_vectors[0],
            acc_vectors[1],
            acc_vectors[2],
            acc_vectors[3],
            acc_vectors[4],
            acc_vectors[5],
        ),
        "tensor",
    )
    owned = (
        lax.psum_scatter(acc_attn, "dp", scatter_dimension=1, tiled=True),
        lax.psum_scatter(acc_proj, "dp", scatter_dimension=1, tiled=True),
        lax.psum_scatter(acc_up, "dp", scatter_dimension=0, tiled=True),
        lax.psum_scatter(acc_down, "dp", scatter_dimension=1, tiled=True),
        lax.psum_scatter(summed[0], "dp", scatter_dimension=0, tiled=True),
        lax.psum_scatter(summed[1], "dp", scatter_dimension=0, tiled=True),
        lax.psum_scatter(summed[2], "dp", scatter_dimension=0, tiled=True),
        lax.psum_scatter(summed[3], "dp", scatter_dimension=0, tiled=True),
        lax.psum_scatter(summed[4], "dp", scatter_dimension=0, tiled=True),
        lax.psum_scatter(summed[5], "dp", scatter_dimension=0, tiled=True),
    )
    bias_sums = lax.psum((acc_attn_bias, acc_up_bias), "dp")
    block_out = jnp.concatenate(block_parts, axis=1)
    input_grad = jnp.concatenate(input_parts, axis=1)
    return (
        block_out,
        input_grad,
        owned[4],
        owned[5],
        owned[0],
        bias_sums[0],
        owned[1],
        owned[6],
        owned[7],
        owned[8],
        owned[2],
        bias_sums[1],
        owned[3],
        owned[9],
    )


def solution(mesh):
    return jax.shard_map(
        per_device,
        mesh=mesh,
        in_specs=(
            P("tensor", "dp", None),
            P("tensor", "dp", None),
            P("dp", None),
            P("dp"),
            P("dp"),
            P("dp"),
            P(None, "dp", "tensor"),
            P(None, "tensor"),
            P("tensor", "dp"),
            P("dp"),
            P("dp"),
            P("dp"),
            P("dp", "tensor"),
            P("tensor"),
            P("tensor", "dp"),
            P("dp"),
        ),
        out_specs=(
            P("tensor", "dp", None),
            P("tensor", "dp", None),
            P("dp"),
            P("dp"),
            P(None, "dp", "tensor"),
            P(None, "tensor"),
            P("tensor", "dp"),
            P("dp"),
            P("dp"),
            P("dp"),
            P("dp", "tensor"),
            P("tensor"),
            P("tensor", "dp"),
            P("dp"),
        ),
        check_vma=False,
    )
```

profile of v0, /device:TPU:0, one launch (start us, length us, event | category | flops | bytes accessed | tf_op | source)
XLA Modules:
  0.0 1428.0 jit_solution(13615151279646853309)
XLA Ops:
  7.2 3.1 convert_reduce_fusion.11
  10.4 10.3 all-gather
  20.7 8.6 all-gather.1
  29.3 5.2 multiply_reduce_fusion.13
  39.6 9.6 all_gather.68
  49.2 40.0 %all-gather.28.cloned.1.call-done = bf16[584,1,1024]{2,1,0:T(2,128)(2,1)} async-done(((bf16[146,1,1024]{2,1,0:T(2,128)(2,1)}), bf16[584,1,1024]{2,1,0:T(2,128)(2,1)}) %all-gather.28.cloned.1.call-update) | async-done | bytes 1196048 | tf_op jit(solution)/shard_map/all_gather | solution.py:96
  89.3 26.4 %all-gather.20.cloned.1.call-done = bf16[3,1024,256]{2,1,0:T(8,128)(2,1)} async-done(((bf16[3,128,256]{2,1,0:T(8,128)(2,1)}), bf16[3,1024,256]{2,1,0:T(8,128)(2,1)}) %all-gather.20.cloned.1.call-update) | async-done | bytes 1572880 | tf_op jit(solution)/shard_map/all_gather | solution.py:68
  115.7 3.3 convolution_bitcast_fusion.6
  119.1 49.8 %all-gather.18.cloned.1.call-done = bf16[584,1,1024]{2,1,0:T(2,128)(2,1)} async-done(((bf16[146,1,1024]{2,1,0:T(2,128)(2,1)}), bf16[584,1,1024]{2,1,0:T(2,128)(2,1)}) %all-gather.18.cloned.1.call-update) | async-done | bytes 1196048 | tf_op jit(solution)/shard_map/all_gather | solution.py:96
  168.9 3.3 convolution_bitcast_fusion.7
  185.2 3.9 copy.127
  194.9 3.9 copy.133
  199.5 8.7 all-gather.2
  208.3 8.7 all-gather.3
  216.9 7.8 all-gather.4
  226.0 146.3 %all-reduce.30.cloned.1.call-done = (f32[584,1,1024]{2,1,0:T(1,128)}, f32[584,1,1024]{2,1,0:T(1,128)}) async-done(((f32[584,1,1024]{2,1,0:T(1,128)}, f32[584,1,1024]{2,1,0:T(1,128)}), (f32[584,1,1024]{2,1,0:T(1,128)}, f32[584,1,1024]{2,1,0:T(1,128)})) %all-reduce.30.cloned.1.call-update) | async-done | bytes 4784144
  372.3 4.0 fusion.112
  385.8 15.3 %all-gather.24.cloned.1.call-done = bf16[1024,1024]{1,0:T(8,128)(2,1)} async-done(((bf16[128,1024]{1,0:T(8,128)(2,1)}), bf16[1024,1024]{1,0:T(8,128)(2,1)}) %all-gather.24.cloned.1.call-update) | async-done | bytes 2097168 | tf_op jit(solution)/shard_map/all_gather | solution.py:70
  401.1 52.6 %all-gather.30.cloned.1.call-done = bf16[584,1,1024]{2,1,0:T(2,128)(2,1)} async-done(((bf16[146,1,1024]{2,1,0:T(2,128)(2,1)}), bf16[584,1,1024]{2,1,0:T(2,128)(2,1)}) %all-gather.30.cloned.1.call-update) | async-done | bytes 1196048 | tf_op jit(solution)/shard_map/all_gather | solution.py:137
  453.7 5.1 fusion.57
  458.8 47.0 %all-gather.22.cloned.1.call-done = bf16[584,1,1024]{2,1,0:T(2,128)(2,1)} async-done(((bf16[146,1,1024]{2,1,0:T(2,128)(2,1)}), bf16[584,1,1024]{2,1,0:T(2,128)(2,1)}) %all-gather.22.cloned.1.call-update) | async-done | bytes 1196048 | tf_op jit(solution)/shard_map/all_gather | solution.py:137
  505.7 16.0 %multiply_convert_fusion.3 = (bf16[584,1024]{1,0:T(8,128)(2,1)}, f32[584,1024]{1,0:T(8,128)}, bf16[584,1024]{1,0:T(8,128)(2,1)}, f32[584,1024]{1,0:T(8,128)}, f32[584,1024]{1,0:T(8,128)}) fusion(f32[1024]{0:T(1024)S(1)} %convert_element_type.338, f32[584,1024]{1,0:T(8,128)} %fusion.57, bf16[1024,1024]{1,0:T(8,128)(2,1)} %all-gather.24.cloned.1.call-done, ...), kind=kOutput, calls=%fused_computation.44 | convolution fusion | flops 1303674880 | bytes 15257600 | tf_op jit(solution)/shard_map/sid,df->sif/dot_general | solution.py:139
  521.8 13.0 all-gather.26.cloned.1.call-done
  534.8 4.6 fusion.26
  539.4 2.5 fusion.27
  541.9 48.2 %fusion.106 = (bf16[152,1024]{1,0:T(8,128)(2,1)S(1)}, bf16[152,1024]{1,0:T(8,128)(2,1)}) fusion(bf16[584,1,1024]{2,0,1:T(8,128)(2,1)} %fusion.27, bf16[584,1,1024]{2,0,1:T(8,128)(2,1)} %fusion.26), kind=kCustom, calls=%all-reduce-scatter.2 | all-reduce-scatter fusion | flops 1245185 | bytes 3015168
  590.9 3.4 collective-permute-start
  595.6 8.7 all-gather.5
  606.9 3.3 concatenate.10
  612.0 2.9 concatenate.11
  615.9 8.2 multiply_convert_fusion.5
  628.0 47.2 %all-gather.32.cloned.1.call-done = bf16[584,1,1024]{2,1,0:T(2,128)(2,1)} async-done(((bf16[146,1,1024]{2,1,0:T(2,128)(2,1)}), bf16[584,1,1024]{2,1,0:T(2,128)(2,1)}) %all-gather.32.cloned.1.call-update) | async-done | bytes 1196048 | tf_op jit(solution)/shard_map/all_gather | solution.py:157
  675.2 6.1 convert_reduce_fusion.1
  683.8 3.9 copy.135
  687.6 38.9 %all-gather.36.cloned.1.call-done = bf16[584,1,1024]{2,1,0:T(2,128)(2,1)} async-done(((bf16[146,1,1024]{2,1,0:T(2,128)(2,1)}), bf16[584,1,1024]{2,1,0:T(2,128)(2,1)}) %all-gather.36.cloned.1.call-update) | async-done | bytes 1196048 | tf_op jit(solution)/shard_map/all_gather | solution.py:157
  726.5 6.1 convert_reduce_fusion
  735.1 3.8 copy.144
  739.2 173.2 %all-reduce.28.cloned.1.call-done = (f32[584,1,1024]{2,1,0:T(1,128)}, f32[584,1,1024]{2,1,0:T(1,128)}) async-done(((f32[584,1,1024]{2,1,0:T(1,128)}, f32[584,1,1024]{2,1,0:T(1,128)}), (f32[584,1,1024]{2,1,0:T(1,128)}, f32[584,1,1024]{2,1,0:T(1,128)})) %all-reduce.28.cloned.1.call-update) | async-done | bytes 4784144
  912.3 5.0 multiply_reduce_fusion.3
  917.4 6.1 fusion.109
  929.7 46.1 %all-gather.34.cloned.1.call-done = bf16[584,1,1024]{2,1,0:T(2,128)(2,1)} async-done(((bf16[146,1,1024]{2,1,0:T(2,128)(2,1)}), bf16[584,1,1024]{2,1,0:T(2,128)(2,1)}) %all-gather.34.cloned.1.call-update) | async-done | bytes 1196048 | tf_op jit(solution)/shard_map/all_gather | solution.py:183
  975.7 2.9 convolution_convert_fusion.3
  979.8 4.4 multiply_reduce_fusion.1
  990.3 37.4 %all-gather.38.cloned.1.call-done = bf16[584,1,1024]{2,1,0:T(2,128)(2,1)} async-done(((bf16[146,1,1024]{2,1,0:T(2,128)(2,1)}), bf16[584,1,1024]{2,1,0:T(2,128)(2,1)}) %all-gather.38.cloned.1.call-update) | async-done | bytes 1196048 | tf_op jit(solution)/shard_map/all_gather | solution.py:183
  1030.2 3.9 convert_reduce_fusion.2
  1034.1 4.2 multiply_reduce_fusion
  1042.4 3.8 fusion.65
  1046.2 3.3 add_bitcast_fusion
  1049.6 2.5 convolution_bitcast_fusion.2
  1052.2 3.9 copy.143
  1057.2 3.8 copy.152
  1062.4 3.7 fusion.50
  1066.1 4.0 convolution_add_fusion
  1071.4 3.8 fusion.61
  1075.2 4.0 convolution_add_fusion.1
  1087.9 6.9 reduce-scatter.11.cloned.1.call-done
  1096.7 174.9 %all-reduce.26.cloned.1.call-done = (f32[584,1,1024]{2,1,0:T(1,128)}, f32[584,1,1024]{2,1,0:T(1,128)}) async-done(((f32[584,1,1024]{2,1,0:T(1,128)}, f32[584,1,1024]{2,1,0:T(1,128)}), (f32[584,1,1024]{2,1,0:T(1,128)}, f32[584,1,1024]{2,1,0:T(1,128)})) %all-reduce.26.cloned.1.call-update) | async-done | bytes 4784144
  1271.7 5.0 multiply_reduce_fusion.5
  1276.7 25.3 %all-reduce.16 = (f32[1024]{0:T(1024)S(1)}, f32[1024]{0:T(1024)S(1)}, f32[2,256]{1,0:T(2,128)}, f32[1024]{0:T(1024)S(1)}, f32[1024]{0:T(1024)S(1)}, /*index=5*/f...) all-reduce(f32[1024]{0:T(1024)S(1)} %add.380, ...), channel_id=10, replica_groups=mesh['dp'=8,'tensor'=4] {'dp'}, use_global_device_ids=true, to_apply=%region_33.34.clone | all-reduce | flops 7680 | bytes 61440
  1302.4 10.2 all-reduce.17
  1312.7 5.4 fusion.107
  1321.6 4.2 reduce-scatter.17.cloned.1.call-done
  1325.8 55.5 %reduce-scatter.15.cloned.1.call-done = f32[128,1024]{1,0:T(8,128)} async-done(((f32[1024,1024]{1,0:T(8,128)}), f32[128,1024]{1,0:T(8,128)}) %reduce-scatter.15.cloned.1.call-update) | async-done | bytes 524304 | tf_op jit(solution)/shard_map/reduce_scatter | solution.py:244
  1381.3 39.6 %reduce-scatter.13.cloned.1.call-done = f32[256,128]{1,0:T(8,128)} async-done(((f32[256,1024]{1,0:T(8,128)}), f32[256,128]{1,0:T(8,128)}) %reduce-scatter.13.cloned.1.call-update) | async-done | bytes 131088 | tf_op jit(solution)/shard_map/reduce_scatter | solution.py:243
  (290 shorter events, 86.9 us)
Async XLA Ops:
  7.2 82.1 %all-gather.28.cloned.1.call-start = ((), (), s32[]{:S(2)}) async-start(), calls=%async_computation.9 | async-start | bytes 2990080 | tf_op jit(solution)/shard_map/all_gather | solution.py:96
  20.7 17.1 %copy-start.38 = (f32[8,1,128]{2,1,0:T(1,128)}, f32[8,1,128]{2,1,0:T(1,128)S(1)}, u32[]{:S(2)}) copy-start(f32[8,1,128]{2,1,0:T(1,128)S(1)} %convert_element_type.404) | copy-start | bytes 12292
  34.5 84.5 %copy-start.48 = (f32[146]{0:T(256)}, f32[146]{0:T(256)S(1)}, u32[]{:S(2)}) copy-start(f32[146]{0:T(256)S(1)} %get-tuple-element.152) | copy-start | bytes 1756
  34.5 4.8 copy-start.52
  34.5 5.0 copy-start.45
  34.6 5.0 copy-start.40
  37.8 77.9 %all-gather.20.cloned.1.call-start = ((), (), s32[]{:S(2)}) async-start(), calls=%async_computation.5 | async-start | bytes 1769472 | tf_op jit(solution)/shard_map/all_gather | solution.py:68
  38.5 130.4 %all-gather.18.cloned.1.call-start = ((), (), s32[]{:S(2)}) async-start(), calls=%async_computation.4 | async-start | bytes 2990080 | tf_op jit(solution)/shard_map/all_gather | solution.py:96
  39.3 333.0 %all-reduce.30.cloned.1.call-start = ((), (), s32[]{:S(2)}) async-start(), calls=%async_computation.21 | async-start | bytes 9568256
  49.2 145.2 %copy-start.15 = (bf16[256,1024]{1,0:T(8,128)(2,1)}, bf16[256,1024]{1,0:T(8,128)(2,1)S(1)}, u32[]{:S(2)}) copy-start(bf16[256,1024]{1,0:T(8,128)(2,1)S(1)} %all_gather.68) | copy-start | bytes 1572868
  174.5 17.1 %copy-start.19 = (f32[1,584,1,256]{1,3,2,0:T(8,128)}, f32[1,584,1,256]{1,3,2,0:T(8,128)S(1)}, u32[]{:S(2)}) copy-start(f32[1,584,1,256]{1,3,2,0:T(8,128)S(1)} %copy.129) | copy-start | bytes 1794052
  175.9 5.0 copy-start.17
  184.7 4.4 copy-start.25
  194.4 4.5 copy-start.27
  198.8 9.4 copy-start.54
  198.8 18.1 %copy-start.55 = (bf16[128]{0:T(256)(128)(2,1)S(1)}, bf16[128]{0:T(256)(128)(2,1)}, u32[]{:S(2)}) copy-start(bf16[128]{0:T(256)(128)(2,1)} %param.27) | copy-start | bytes 772
  198.8 25.9 %copy-start.51 = (u32[32]{0:T(128)S(1)}, u32[32]{0:T(128)}, u32[]{:S(2)}) copy-start(u32[32]{0:T(128)} %constant.109) | copy-start | bytes 388
  198.8 173.4 %copy-start.2 = (bf16[146,2,1024]{2,1,0:T(2,128)(2,1)S(1)}, bf16[146,2,1024]{2,1,0:T(2,128)(2,1)}, u32[]{:S(2)}) copy-start(bf16[146,2,1024]{2,1,0:T(2,128)(2,1)} %param.16) | copy-start | bytes 1794052
  198.9 202.2 %all-gather.24.cloned.1.call-start = ((), (), s32[]{:S(2)}) async-start(), calls=%async_computation.7 | async-start | bytes 2359296 | tf_op jit(solution)/shard_map/all_gather | solution.py:70
  199.5 254.2 %all-gather.30.cloned.1.call-start = ((), (), s32[]{:S(2)}) async-start(), calls=%async_computation.10 | async-start | bytes 2990080 | tf_op jit(solution)/shard_map/all_gather | solution.py:137
  376.3 6.4 copy-start.13
  376.3 6.4 copy-start.14
  378.3 7.4 copy-start.50
  382.7 123.1 %all-gather.22.cloned.1.call-start = ((), (), s32[]{:S(2)}) async-start(), calls=%async_computation.6 | async-start | bytes 2990080 | tf_op jit(solution)/shard_map/all_gather | solution.py:137
  383.4 151.4 %all-gather.26.cloned.1.call-start = ((), (), s32[]{:S(2)}) async-start(), calls=%async_computation.8 | async-start | bytes 2359296 | tf_op jit(solution)/shard_map/all_gather | solution.py:71
  384.2 291.0 %all-gather.32.cloned.1.call-start = ((), (), s32[]{:S(2)}) async-start(), calls=%async_computation.11 | async-start | bytes 2990080 | tf_op jit(solution)/shard_map/all_gather | solution.py:157
  534.8 4.6 copy-start.30
  534.8 4.6 copy-start.59
  541.9 53.6 %copy-start.56 = (bf16[128]{0:T(256)(128)(2,1)S(1)}, bf16[128]{0:T(256)(128)(2,1)}, u32[]{:S(2)}) copy-start(bf16[128]{0:T(256)(128)(2,1)} %param.31) | copy-start | bytes 772
  590.9 16.0 %collective-permute-start = (bf16[18,1024]{1,0:T(8,128)(2,1)S(1)}, bf16[18,1024]{1,0:T(8,128)(2,1)S(1)}, u32[]{:S(2)}, u32[]{:S(2)}) collective-permute-start(bf16[18,1024]{1,0:T(8,128)(2,1)S(1)} %slice.94), channel_id=1, source_target_pairs={{0,1},{1,2},{2,3},{4,5},{5,6},{6,7},{8,9},{9,10},{10,11},{12,13},{... | collective-permute-start | bytes 110600
  605.0 7.0 collective-permute-start.1
  624.1 57.2 %copy-start.9 = (f32[146,1,1024]{2,1,0:T(1,128)}, f32[146,1,1024]{2,1,0:T(1,128)S(1)}, u32[]{:S(2)}) copy-start(f32[146,1,1024]{2,1,0:T(1,128)S(1)} %get-tuple-element.173) | copy-start | bytes 1794052
  626.2 100.4 %all-gather.36.cloned.1.call-start = ((), (), s32[]{:S(2)}) async-start(), calls=%async_computation.13 | async-start | bytes 2990080 | tf_op jit(solution)/shard_map/all_gather | solution.py:157
  627.5 284.9 %all-reduce.28.cloned.1.call-start = ((), (), s32[]{:S(2)}) async-start(), calls=%async_computation.20 | async-start | bytes 9568256
  675.2 7.2 copy-start.57
  726.5 7.1 copy-start.58
  738.9 236.8 %all-gather.34.cloned.1.call-start = ((), (), s32[]{:S(2)}) async-start(), calls=%async_computation.12 | async-start | bytes 2990080 | tf_op jit(solution)/shard_map/all_gather | solution.py:183
  917.3 6.1 copy-start.12
  925.5 50.2 %copy-start.16 = (bf16[256,1024]{1,0:T(8,128)(2,1)S(1)}, bf16[256,1024]{1,0:T(8,128)(2,1)}, u32[]{:S(2)}) copy-start(bf16[256,1024]{1,0:T(8,128)(2,1)} %copy-done.15) | copy-start | bytes 1572868
  925.5 102.2 %all-gather.38.cloned.1.call-start = ((), (), s32[]{:S(2)}) async-start(), calls=%async_computation.14 | async-start | bytes 2990080 | tf_op jit(solution)/shard_map/all_gather | solution.py:183
  929.6 165.2 %reduce-scatter.11.cloned.1.call-start = ((), (), s32[]{:S(2)}) async-start(), calls=%async_computation.15 | async-start | bytes 3538944 | tf_op jit(solution)/shard_map/reduce_scatter | solution.py:242
  979.8 4.5 slice-start.2
  979.8 5.0 slice-start.3
  1030.1 4.0 copy-start.20
  1030.1 8.2 slice-start
  1034.1 4.2 slice-start.1
  1042.4 3.8 copy-start.34
  1049.6 222.0 %all-reduce.26.cloned.1.call-start = ((), (), s32[]{:S(2)}) async-start(), calls=%async_computation.19 | async-start | bytes 9568256
  1052.2 3.9 copy-start.60
  1061.1 5.0 copy-start.31
  1061.1 264.7 %reduce-scatter.17.cloned.1.call-start = ((), (), s32[]{:S(2)}) async-start(), calls=%async_computation.18 | async-start | bytes 4718592 | tf_op jit(solution)/shard_map/reduce_scatter | solution.py:245
  1070.1 5.1 copy-start.33
  1070.1 311.2 %reduce-scatter.15.cloned.1.call-start = ((), (), s32[]{:S(2)}) async-start(), calls=%async_computation.17 | async-start | bytes 4718592 | tf_op jit(solution)/shard_map/reduce_scatter | solution.py:244
  1079.3 4.4 copy-start.26
  1079.3 6.9 copy-start.28
  1079.3 341.6 %reduce-scatter.13.cloned.1.call-start = ((), (), s32[]{:S(2)}) async-start(), calls=%async_computation.16 | async-start | bytes 1179648 | tf_op jit(solution)/shard_map/reduce_scatter | solution.py:243
  1086.2 185.4 %copy-start.4 = (f32[146,1,1024]{2,1,0:T(1,128)S(1)}, f32[146,1,1024]{2,1,0:T(1,128)}, u32[]{:S(2)}) copy-start(f32[146,1,1024]{2,1,0:T(1,128)} %copy-done.3) | copy-start | bytes 1794052
  1086.2 185.4 %copy-start.6 = (f32[146,1,1024]{2,1,0:T(1,128)S(1)}, f32[146,1,1024]{2,1,0:T(1,128)}, u32[]{:S(2)}) copy-start(f32[146,1,1024]{2,1,0:T(1,128)} %copy-done.5) | copy-start | bytes 1794052
  1086.2 185.4 %copy-start.39 = (f32[8,1,128]{2,1,0:T(1,128)S(1)}, f32[8,1,128]{2,1,0:T(1,128)}, u32[]{:S(2)}) copy-start(f32[8,1,128]{2,1,0:T(1,128)} %copy-done.38) | copy-start | bytes 12292
  1086.2 185.4 %copy-start.42 = (f32[146]{0:T(256)S(1)}, f32[146]{0:T(256)}, u32[]{:S(2)}) copy-start(f32[146]{0:T(256)} %copy-done.41) | copy-start | bytes 1756
  1086.2 185.4 %copy-start.44 = (f32[146]{0:T(256)S(1)}, f32[146]{0:T(256)}, u32[]{:S(2)}) copy-start(f32[146]{0:T(256)} %copy-done.43) | copy-start | bytes 1756
  1087.9 188.8 %copy-start.49 = (f32[146]{0:T(256)S(1)}, f32[146]{0:T(256)}, u32[]{:S(2)}) copy-start(f32[146]{0:T(256)} %copy-done.48) | copy-start | bytes 1756
  1087.9 188.8 %copy-start.47 = (f32[146]{0:T(256)S(1)}, f32[146]{0:T(256)}, u32[]{:S(2)}) copy-start(f32[146]{0:T(256)} %copy-done.46) | copy-start | bytes 1756
  1312.7 6.1 copy-start.8
  (25 other events, 45.0 us)
Sparse Core Ops, SparseCore 0:
  37.9 51.3 all-gather.27
  91.2 24.4 all-gather.19
  117.8 51.0 all-gather.17
  199.0 173.2 all-reduce.29
  374.2 26.8 all-gather.23
  402.6 51.0 all-gather.29
  455.9 49.8 all-gather.21
  507.8 26.9 all-gather.25
  626.3 48.8 all-gather.31
  676.6 49.8 all-gather.35
  739.1 173.2 all-reduce.27
  925.7 50.0 all-gather.33
  977.8 49.8 all-gather.37
  1049.7 45.0 reduce-scatter.10
  1097.2 174.4 all-reduce.25
  1275.4 50.3 reduce-scatter.16
  1329.9 51.3 reduce-scatter.14
  1384.9 35.9 reduce-scatter.12
where the time goes:
time: 1430 us
  waiting for transfers between devices  1020 us (71%)
  blocking collectives  146 us (10%)
  matrix products  110 us (8%)
  other arithmetic  69.8 us (5%)
  local copies, waits for them, and re-layouts  58.6 us (4%)
  between operations  18.3 us (1%)
    unnamed x23, waiting for transfers between devices  498 us
    all_gather x2, waiting for transfers between devices, per_device(): normed2_all = lax.all_gather(normed2, 'tensor', axis=0, tiled=True)  99.5 us
    all_gather x2, waiting for transfers between devices, per_device(): normed_all = lax.all_gather(normed, 'tensor', axis=0, tiled=True)  89.8 us
    all_gather x2, waiting for transfers between devices, per_device(): mlp_grad_all = lax.all_gather(mlp_grad, 'tensor', axis=0, tiled=True)  86.1 us
    all_gather x2, waiting for transfers between devices, per_device(): branch_all = lax.all_gather(branch_grad, 'tensor', axis=0, tiled=True)  83.5 us
    unnamed x2, blocking collectives  73.4 us
    reduce_scatter x1, waiting for transfers between devices, per_device(): lax.psum_scatter(acc_up, 'dp', scatter_dimension=0, tiled=True)  55.5 us
    reduce_scatter x1, waiting for transfers between devices, per_device(): lax.psum_scatter(acc_proj, 'dp', scatter_dimension=1, tiled=True)  39.6 us
  transfers between devices with their start and end apart: 20, of which 18 were waited for; matrix products, arithmetic and copies ran while one was open for 9% of the time, Pallas kernels for 0%

commit v1 on v0

--- a/solution.py
+++ b/solution.py
@@ -180,7 +180,25 @@
         resid_grad = outer + resid_part
         branch_grad = resid_grad.astype(bf16)
         acc_vectors[2] = acc_vectors[2] + jnp.sum(branch_grad.astype(f32), axis=(0, 1))
-        branch_all = lax.all_gather(branch_grad, "tensor", axis=0, tiled=True)
+        ways, here, step = (lax.axis_size("tensor"), lax.axis_index("tensor"), branch_grad.shape[0])
+        lengths = [n * ways if d == 0 else n for d, n in enumerate(branch_grad.shape)]
+        full = lax.dynamic_update_slice_in_dim(
+            jnp.zeros(lengths, branch_grad.dtype), branch_grad, here * step, axis=0
+        )
+        going_up = going_down = branch_grad
+        for far in range(1, ways // 2 + 1):
+            going_up = lax.ppermute(going_up, "tensor", [(d, (d + 1) % ways) for d in range(ways)])
+            full = lax.dynamic_update_slice_in_dim(
+                full, going_up, (here - far) % ways * step, axis=0
+            )
+            if 2 * far < ways:
+                going_down = lax.ppermute(
+                    going_down, "tensor", [(d, (d - 1) % ways) for d in range(ways)]
+                )
+                full = lax.dynamic_update_slice_in_dim(
+                    full, going_down, (here + far) % ways * step, axis=0
+                )
+        branch_all = full
         acc_proj = acc_proj + jnp.einsum(
             "sie,sid->ed", attended, branch_all, preferred_element_type=f32
         )

time: 1430 us -> 1340 us (0.937)
  waiting for transfers between devices: 1020 us -> 857 us
  other arithmetic: 69.8 us -> 24.3 us
  local copies, waits for them, and re-layouts: 58.6 us -> 104 us
  blocking collectives: 146 us -> 186 us
  starting transfers between devices: 7.04 us -> 36.5 us
    unnamed x23 -> x21, waiting for transfers between devices: 498 us -> 407 us
    all_gather x2 -> x0, waiting for transfers between devices: 83.5 us -> none  [per_device(): branch_all = lax.all_gather(branch_grad, 'tensor', axis=0, tiled=True)]
    reduce_scatter x1, waiting for transfers between devices: 4.22 us -> 55.5 us  [per_device(): lax.psum_scatter(acc_down, 'dp', scatter_dimension=1, tiled=True)]
    reduce_scatter x1, waiting for transfers between devices: 55.5 us -> 9.88 us  [per_device(): lax.psum_scatter(acc_up, 'dp', scatter_dimension=0, tiled=True)]
    unnamed x2, blocking collectives: 73.4 us -> 113 us
    dynamic_update_slice x0 -> x8, local copies, waits for them, and re-layouts: none -> 21.6 us  [the longest x4 11.3 us: per_device(): lax.dynamic_update_slice_in_dim(full, going_up, (here - far) % ways * ste...]
    reduce_sum x4, other arithmetic: 18.6 us -> 2.29 us  [layer_norm(): center = values - jnp.mean(values, axis=-1, keepdims=True)]
    ppermute x0 -> x6, starting transfers between devices: none -> 16.2 us  [the longest x4 8.53 us: per_device(): lax.ppermute(going_up, 'tensor', [(d, (d + 1) % ways) for d in range(ways)])]
  transfers between devices with their start and end apart: 20 -> 24, of which waited for: 18 -> 18; matrix products, arithmetic and copies ran while one was open for 9% -> 18% of each run, Pallas kernels for 0% -> 0%
where the time goes in v1:
time: 1340 us
  waiting for transfers between devices  857 us (64%)
  blocking collectives  186 us (14%)
  matrix products  111 us (8%)
  local copies, waits for them, and re-layouts  104 us (8%)
  starting transfers between devices  36.5 us (3%)
  other arithmetic  24.3 us (2%)
  between operations  18.3 us (1%)
    unnamed x21, waiting for transfers between devices  407 us
    unnamed x2, blocking collectives  113 us
    all_gather x2, waiting for transfers between devices, per_device(): normed2_all = lax.all_gather(normed2, 'tensor', axis=0, tiled=True)  100 us
    all_gather x2, waiting for transfers between devices, per_device(): normed_all = lax.all_gather(normed, 'tensor', axis=0, tiled=True)  88.8 us
    all_gather x2, waiting for transfers between devices, per_device(): mlp_grad_all = lax.all_gather(mlp_grad, 'tensor', axis=0, tiled=True)  74.9 us
    reduce_scatter x1, waiting for transfers between devices, per_device(): lax.psum_scatter(acc_down, 'dp', scatter_dimension=1, tiled=True)  55.5 us
    reduce_scatter x1, waiting for transfers between devices, per_device(): lax.psum_scatter(acc_proj, 'dp', scatter_dimension=1, tiled=True)  39.6 us
    all_gather x1, waiting for transfers between devices, per_device(): lax.all_gather(down_weight, 'dp', axis=1, tiled=True)  29.1 us
  transfers between devices with their start and end apart: 24, of which 18 were waited for; matrix products, arithmetic and copies ran while one was open for 18% of the time, Pallas kernels for 0%

profile of v1, /device:TPU:0, one launch (start us, length us, event | category | flops | bytes accessed | tf_op | source)
XLA Modules:
  0.0 1335.9 jit_solution(11904981683167045099)
XLA Ops:
  11.6 10.2 all-gather
  21.8 8.7 all-gather.1
  34.5 9.2 all_gather.62
  43.7 39.9 %all-gather.16.cloned.1.call-done = bf16[584,1,1024]{2,1,0:T(2,128)(2,1)} async-done(((bf16[146,1,1024]{2,1,0:T(2,128)(2,1)}), bf16[584,1,1024]{2,1,0:T(2,128)(2,1)}) %all-gather.16.cloned.1.call-update) | async-done | bytes 1196048 | tf_op jit(solution)/shard_map/all_gather | solution.py:96
  83.6 26.4 %all-gather.18.cloned.1.call-done = bf16[3,1024,256]{2,1,0:T(8,128)(2,1)} async-done(((bf16[3,128,256]{2,1,0:T(8,128)(2,1)}), bf16[3,1024,256]{2,1,0:T(8,128)(2,1)}) %all-gather.18.cloned.1.call-update) | async-done | bytes 1572880 | tf_op jit(solution)/shard_map/all_gather | solution.py:68
  110.0 3.3 convolution_bitcast_fusion.7
  114.2 49.0 %all-gather.26.cloned.1.call-done = bf16[584,1,1024]{2,1,0:T(2,128)(2,1)} async-done(((bf16[146,1,1024]{2,1,0:T(2,128)(2,1)}), bf16[584,1,1024]{2,1,0:T(2,128)(2,1)}) %all-gather.26.cloned.1.call-update) | async-done | bytes 1196048 | tf_op jit(solution)/shard_map/all_gather | solution.py:96
  163.2 3.3 convolution_bitcast_fusion.6
  176.0 3.9 copy.129
  188.7 3.9 copy.138
  193.4 8.7 all-gather.2
  202.1 8.7 all-gather.3
  210.8 7.8 all-gather.4
  219.8 146.3 %all-reduce.30.cloned.1.call-done = (f32[584,1,1024]{2,1,0:T(1,128)}, f32[584,1,1024]{2,1,0:T(1,128)}) async-done(((f32[584,1,1024]{2,1,0:T(1,128)}, f32[584,1,1024]{2,1,0:T(1,128)}), (f32[584,1,1024]{2,1,0:T(1,128)}, f32[584,1,1024]{2,1,0:T(1,128)})) %all-reduce.30.cloned.1.call-update) | async-done | bytes 4784144
  381.6 13.3 all-gather.22.cloned.1.call-done
  394.9 53.1 %all-gather.28.cloned.1.call-done = bf16[584,1,1024]{2,1,0:T(2,128)(2,1)} async-done(((bf16[146,1,1024]{2,1,0:T(2,128)(2,1)}), bf16[584,1,1024]{2,1,0:T(2,128)(2,1)}) %all-gather.28.cloned.1.call-update) | async-done | bytes 1196048 | tf_op jit(solution)/shard_map/all_gather | solution.py:137
  448.1 5.2 fusion.52
  453.2 46.9 %all-gather.20.cloned.1.call-done = bf16[584,1,1024]{2,1,0:T(2,128)(2,1)} async-done(((bf16[146,1,1024]{2,1,0:T(2,128)(2,1)}), bf16[584,1,1024]{2,1,0:T(2,128)(2,1)}) %all-gather.20.cloned.1.call-update) | async-done | bytes 1196048 | tf_op jit(solution)/shard_map/all_gather | solution.py:137
  500.1 16.2 %multiply_convert_fusion.3 = (bf16[584,1024]{1,0:T(8,128)(2,1)}, f32[584,1024]{1,0:T(8,128)}, bf16[584,1024]{1,0:T(8,128)(2,1)}, f32[584,1024]{1,0:T(8,128)}, f32[584,1024]{1,0:T(8,128)}) fusion(f32[1024]{0:T(1024)S(1)} %convert_element_type.338, f32[584,1024]{1,0:T(8,128)} %fusion.52, bf16[1024,1024]{1,0:T(8,128)(2,1)} %all-gather.22.cloned.1.call-done, ...), kind=kOutput, calls=%fused_computation.44 | convolution fusion | flops 1303674880 | bytes 15257600 | tf_op jit(solution)/shard_map/sid,df->sif/dot_general | solution.py:139
  516.3 35.3 %all-gather.30.cloned.1.call-done = bf16[584,1,1024]{2,1,0:T(2,128)(2,1)} async-done(((bf16[146,1,1024]{2,1,0:T(2,128)(2,1)}), bf16[584,1,1024]{2,1,0:T(2,128)(2,1)}) %all-gather.30.cloned.1.call-update) | async-done | bytes 1196048 | tf_op jit(solution)/shard_map/all_gather | solution.py:157
  551.7 29.1 %all-gather.24.cloned.1.call-done = bf16[1024,1024]{1,0:T(8,128)(2,1)} async-done(((bf16[1024,128]{1,0:T(8,128)(2,1)}), bf16[1024,1024]{1,0:T(8,128)(2,1)}) %all-gather.24.cloned.1.call-update) | async-done | bytes 2097168 | tf_op jit(solution)/shard_map/all_gather | solution.py:71
  580.7 6.7 convert_reduce_fusion.1
  589.9 3.8 copy.143
  593.7 39.5 %all-gather.32.cloned.1.call-done = bf16[584,1,1024]{2,1,0:T(2,128)(2,1)} async-done(((bf16[146,1,1024]{2,1,0:T(2,128)(2,1)}), bf16[584,1,1024]{2,1,0:T(2,128)(2,1)}) %all-gather.32.cloned.1.call-update) | async-done | bytes 1196048 | tf_op jit(solution)/shard_map/all_gather | solution.py:157
  633.3 6.7 convert_reduce_fusion
  642.4 3.9 copy.156
  646.6 4.6 fusion.26
  653.6 88.4 %fusion.117 = (bf16[152,1024]{1,0:T(8,128)(2,1)S(1)}, bf16[152,1024]{1,0:T(8,128)(2,1)}) fusion(bf16[584,1,1024]{2,0,1:T(8,128)(2,1)} %fusion.27, bf16[584,1,1024]{2,0,1:T(8,128)(2,1)} %fusion.26), kind=kCustom, calls=%all-reduce-scatter.2 | all-reduce-scatter fusion | flops 1245185 | bytes 3015168
  743.5 14.4 %collective-permute-start.6 = (bf16[18,1024]{1,0:T(8,128)(2,1)}, bf16[18,1024]{1,0:T(8,128)(2,1)S(1)}, u32[]{:S(2)}, u32[]{:S(2)}) collective-permute-start(bf16[18,1024]{1,0:T(8,128)(2,1)} %slice.94), channel_id=1, source_target_pairs={{0,1},{1,2},{2,3},{4,5},{5,6},{6,7},{8,9},{9,10},{10,11},{12,13},{... | collective-permute-start | bytes 110600
  757.9 4.7 collective-permute-start.7
  762.6 8.8 all-gather.5
  772.2 3.3 concatenate.10
  775.4 2.9 concatenate.11
  778.3 83.0 %all-reduce.28.cloned.1.call-done = (f32[584,1,1024]{2,1,0:T(1,128)}, f32[584,1,1024]{2,1,0:T(1,128)}) async-done(((f32[584,1,1024]{2,1,0:T(1,128)}, f32[584,1,1024]{2,1,0:T(1,128)}), (f32[584,1,1024]{2,1,0:T(1,128)}, f32[584,1,1024]{2,1,0:T(1,128)})) %all-reduce.28.cloned.1.call-update) | async-done | bytes 4784144
  861.3 3.2 fusion.120
  868.9 3.8 collective-permute-start.1
  874.2 3.8 collective-permute-start.4
  878.0 3.0 collective-permute-done
  881.0 4.1 collective-permute-start.2
  888.3 2.8 dynamic_update_slice.36
  891.2 2.7 dynamic_update_slice.33
  898.0 2.9 dynamic_update_slice.34
  900.9 2.8 dynamic_update_slice.38
  903.7 4.4 collective-permute-start.5
  908.1 2.8 dynamic_update_slice.35
  915.3 4.5 multiply_reduce_fusion.1
  927.2 3.2 dynamic_update_slice.39
  932.9 4.4 multiply_reduce_fusion
  949.8 3.6 fusion.60
  953.4 3.3 add_bitcast_fusion
  956.9 2.8 convolution_bitcast_fusion.2
  959.8 3.9 copy.152
  964.8 3.9 copy.165
  968.8 4.2 fusion.56
  973.1 4.0 convolution_add_fusion.1
  977.4 4.5 fusion.45
  982.0 4.1 convolution_add_fusion
  993.8 9.0 reduce-scatter.11.cloned.1.call-done
  1004.7 175.1 %all-reduce.26.cloned.1.call-done = (f32[584,1,1024]{2,1,0:T(1,128)}, f32[584,1,1024]{2,1,0:T(1,128)}) async-done(((f32[584,1,1024]{2,1,0:T(1,128)}, f32[584,1,1024]{2,1,0:T(1,128)}), (f32[584,1,1024]{2,1,0:T(1,128)}, f32[584,1,1024]{2,1,0:T(1,128)})) %all-reduce.26.cloned.1.call-update) | async-done | bytes 4784144
  1185.9 24.8 %all-reduce.16 = (f32[1024]{0:T(1024)S(1)}, f32[1024]{0:T(1024)S(1)}, f32[2,256]{1,0:T(2,128)}, f32[1024]{0:T(1024)S(1)}, f32[1024]{0:T(1024)S(1)}, /*index=5*/f...) all-reduce(f32[1024]{0:T(1024)S(1)} %add.420, ...), channel_id=10, replica_groups=mesh['dp'=8,'tensor'=4] {'dp'}, use_global_device_ids=true, to_apply=%region_33.34.clone | all-reduce | flops 7680 | bytes 61440
  1213.9 10.2 all-reduce.17
  1224.1 9.9 reduce-scatter.15.cloned.1.call-done
  1234.0 55.5 %reduce-scatter.17.cloned.1.call-done = f32[1024,128]{1,0:T(8,128)} async-done(((f32[1024,1024]{1,0:T(8,128)}), f32[1024,128]{1,0:T(8,128)}) %reduce-scatter.17.cloned.1.call-update) | async-done | bytes 524304 | tf_op jit(solution)/shard_map/reduce_scatter | solution.py:263
  1289.5 39.6 %reduce-scatter.13.cloned.1.call-done = f32[256,128]{1,0:T(8,128)} async-done(((f32[256,1024]{1,0:T(8,128)}), f32[256,128]{1,0:T(8,128)}) %reduce-scatter.13.cloned.1.call-update) | async-done | bytes 131088 | tf_op jit(solution)/shard_map/reduce_scatter | solution.py:261
  (367 shorter events, 111.5 us)
Async XLA Ops:
  7.2 14.6 %copy-start.78 = (bf16[128]{0:T(256)(128)(2,1)S(1)}, bf16[128]{0:T(256)(128)(2,1)}, u32[]{:S(2)}) copy-start(bf16[128]{0:T(256)(128)(2,1)} %param.21) | copy-start | bytes 772
  7.2 76.4 %all-gather.16.cloned.1.call-start = ((), (), s32[]{:S(2)}) async-start(), calls=%async_computation.4 | async-start | bytes 2990080 | tf_op jit(solution)/shard_map/all_gather | solution.py:96
  9.9 359.2 %copy-start.2 = (bf16[146,1,1024]{2,0,1:T(8,128)(2,1)}, bf16[146,1,1024]{2,0,1:T(8,128)(2,1)S(1)}, u32[]{:S(2)}) copy-start(bf16[146,1,1024]{2,0,1:T(8,128)(2,1)S(1)} %get-tuple-element.138) | copy-start | bytes 897028
  9.9 24.3 %copy-start.47 = (f32[146]{0:T(256)}, f32[146]{0:T(256)S(1)}, u32[]{:S(2)}) copy-start(f32[146]{0:T(256)S(1)} %broadcast_multiply_fusion.1) | copy-start | bytes 1756
  10.1 24.0 %copy-start.51 = (f32[146]{0:T(256)}, f32[146]{0:T(256)S(1)}, u32[]{:S(2)}) copy-start(f32[146]{0:T(256)S(1)} %fusion.109) | copy-start | bytes 1756
  10.7 358.4 %copy-start.4 = (bf16[146,1,1024]{2,0,1:T(8,128)(2,1)}, bf16[146,1,1024]{2,0,1:T(8,128)(2,1)S(1)}, u32[]{:S(2)}) copy-start(bf16[146,1,1024]{2,0,1:T(8,128)(2,1)S(1)} %get-tuple-element.136) | copy-start | bytes 897028
  10.7 23.5 %copy-start.49 = (f32[146]{0:T(256)}, f32[146]{0:T(256)S(1)}, u32[]{:S(2)}) copy-start(f32[146]{0:T(256)S(1)} %broadcast_multiply_fusion.3) | copy-start | bytes 1756
  10.7 23.6 %copy-start.76 = (bf16[2,256]{1,0:T(2,128)(2,1)S(1)}, bf16[2,256]{1,0:T(2,128)(2,1)}, u32[]{:S(2)}) copy-start(bf16[2,256]{1,0:T(2,128)(2,1)} %param.23) | copy-start | bytes 3076
  10.7 23.8 %copy-start.61 = (s32[2,584]{1,0:T(2,128)S(1)}, s32[2,584]{1,0:T(2,128)}, u32[]{:S(2)}) copy-start(s32[2,584]{1,0:T(2,128)} %param.18) | copy-start | bytes 14020
  10.7 23.8 %copy-start.46 = (bf16[256,128]{1,0:T(8,128)(2,1)S(1)}, bf16[256,128]{1,0:T(8,128)(2,1)}, u32[]{:S(2)}) copy-start(bf16[256,128]{1,0:T(8,128)(2,1)} %param.24) | copy-start | bytes 196612
  11.6 32.2 %copy-start.53 = (f32[146]{0:T(256)}, f32[146]{0:T(256)S(1)}, u32[]{:S(2)}) copy-start(f32[146]{0:T(256)S(1)} %fusion.107) | copy-start | bytes 1756
  21.8 22.0 %copy-start.44 = (f32[8,1,128]{2,1,0:T(1,128)}, f32[8,1,128]{2,1,0:T(1,128)S(1)}, u32[]{:S(2)}) copy-start(f32[8,1,128]{2,1,0:T(1,128)S(1)} %convert_element_type.404) | copy-start | bytes 12292
  32.1 77.9 %all-gather.18.cloned.1.call-start = ((), (), s32[]{:S(2)}) async-start(), calls=%async_computation.5 | async-start | bytes 1769472 | tf_op jit(solution)/shard_map/all_gather | solution.py:68
  32.9 130.4 %all-gather.26.cloned.1.call-start = ((), (), s32[]{:S(2)}) async-start(), calls=%async_computation.9 | async-start | bytes 2990080 | tf_op jit(solution)/shard_map/all_gather | solution.py:96
  34.2 331.9 %all-reduce.30.cloned.1.call-start = ((), (), s32[]{:S(2)}) async-start(), calls=%async_computation.19 | async-start | bytes 9568256
  192.7 9.4 copy-start.80
  192.7 18.1 %copy-start.81 = (bf16[128]{0:T(256)(128)(2,1)S(1)}, bf16[128]{0:T(256)(128)(2,1)}, u32[]{:S(2)}) copy-start(bf16[128]{0:T(256)(128)(2,1)} %param.27) | copy-start | bytes 772
  192.7 25.9 %copy-start.75 = (u32[32]{0:T(128)S(1)}, u32[32]{0:T(128)}, u32[]{:S(2)}) copy-start(u32[32]{0:T(128)} %constant.152) | copy-start | bytes 388
  192.7 202.2 %all-gather.22.cloned.1.call-start = ((), (), s32[]{:S(2)}) async-start(), calls=%async_computation.7 | async-start | bytes 2359296 | tf_op jit(solution)/shard_map/all_gather | solution.py:70
  193.3 254.8 %all-gather.28.cloned.1.call-start = ((), (), s32[]{:S(2)}) async-start(), calls=%async_computation.10 | async-start | bytes 2990080 | tf_op jit(solution)/shard_map/all_gather | solution.py:137
  371.5 128.7 %all-gather.20.cloned.1.call-start = ((), (), s32[]{:S(2)}) async-start(), calls=%async_computation.6 | async-start | bytes 2990080 | tf_op jit(solution)/shard_map/all_gather | solution.py:137
  372.8 178.8 %all-gather.30.cloned.1.call-start = ((), (), s32[]{:S(2)}) async-start(), calls=%async_computation.11 | async-start | bytes 2990080 | tf_op jit(solution)/shard_map/all_gather | solution.py:157
  379.3 201.4 %all-gather.24.cloned.1.call-start = ((), (), s32[]{:S(2)}) async-start(), calls=%async_computation.8 | async-start | bytes 2359296 | tf_op jit(solution)/shard_map/all_gather | solution.py:71
  380.1 253.2 %all-gather.32.cloned.1.call-start = ((), (), s32[]{:S(2)}) async-start(), calls=%async_computation.12 | async-start | bytes 2990080 | tf_op jit(solution)/shard_map/all_gather | solution.py:157
  381.6 479.7 %all-reduce.28.cloned.1.call-start = ((), (), s32[]{:S(2)}) async-start(), calls=%async_computation.18 | async-start | bytes 9568256
  580.7 7.7 copy-start.83
  633.3 7.7 copy-start.84
  646.3 356.5 %reduce-scatter.11.cloned.1.call-start = ((), (), s32[]{:S(2)}) async-start(), calls=%async_computation.13 | async-start | bytes 3538944 | tf_op jit(solution)/shard_map/reduce_scatter | solution.py:260
  646.6 4.6 copy-start.37
  646.6 4.6 copy-start.85
  653.6 109.0 %copy-start.82 = (bf16[128]{0:T(256)(128)(2,1)S(1)}, bf16[128]{0:T(256)(128)(2,1)}, u32[]{:S(2)}) copy-start(bf16[128]{0:T(256)(128)(2,1)} %param.31) | copy-start | bytes 772
  743.5 28.7 %collective-permute-start.6 = (bf16[18,1024]{1,0:T(8,128)(2,1)}, bf16[18,1024]{1,0:T(8,128)(2,1)S(1)}, u32[]{:S(2)}, u32[]{:S(2)}) collective-permute-start(bf16[18,1024]{1,0:T(8,128)(2,1)} %slice.94), channel_id=1, source_target_pairs={{0,1},{1,2},{2,3},{4,5},{5,6},{6,7},{8,9},{9,10},{10,11},{12,13},{... | collective-permute-start | bytes 110600
  757.9 17.5 %collective-permute-start.7 = (bf16[18,1024]{1,0:T(8,128)(2,1)S(1)}, bf16[18,1024]{1,0:T(8,128)(2,1)S(1)}, u32[]{:S(2)}, u32[]{:S(2)}) collective-permute-start(bf16[18,1024]{1,0:T(8,128)(2,1)S(1)} %slice.95), channel_id=1, source_target_pairs={{0,1},{1,2},{2,3},{4,5},{5,6},{6,7},{8,9},{9,10},{10,11},{12,13},{... | collective-permute-start | bytes 110600
  867.3 5.5 copy-start.12
  867.3 5.4 copy-start.64
  868.9 12.2 collective-permute-start
  868.9 28.1 %collective-permute-start.1 = (bf16[146,1,1024]{2,0,1:T(8,128)(2,1)S(1)}, bf16[146,1,1024]{2,0,1:T(8,128)(2,1)}, u32[]{:S(2)}, u32[]{:S(2)}) collective-permute-start(bf16[146,1,1024]{2,0,1:T(8,128)(2,1)S(1)} %get-tuple-element.118), channel_id=1, source_target_pairs={{0,3},{1,0},{2,1},{3,2},{4,7},{5,4},{6,5},{7,6},{8,11},{9,8},{10,9... | collective-permute-start | bytes 897032 | tf_op jit(solution)/shard_map/ppermute | solution.py:195
  872.7 18.4 %copy-start.62 = (f32[146]{0:T(256)}, f32[146]{0:T(256)S(1)}, u32[]{:S(2)}) copy-start(f32[146]{0:T(256)S(1)} %negate_multiply_fusion.3) | copy-start | bytes 1756
  874.2 20.2 %collective-permute-start.3 = (bf16[146,1,1024]{2,0,1:T(8,128)(2,1)}, bf16[146,1,1024]{2,0,1:T(8,128)(2,1)}, u32[]{:S(2)}, u32[]{:S(2)}) collective-permute-start(bf16[146,1,1024]{2,0,1:T(8,128)(2,1)} %get-tuple-element.116), channel_id=1, source_target_pairs={{0,1},{1,2},{2,3},{3,0},{4,5},{5,6},{6,7},{7,4},{8,9},{9,10},{10,1... | collective-permute-start | bytes 897032 | tf_op jit(solution)/shard_map/ppermute | solution.py:190
  874.2 26.7 %collective-permute-start.4 = (bf16[146,1,1024]{2,0,1:T(8,128)(2,1)}, bf16[146,1,1024]{2,0,1:T(8,128)(2,1)}, u32[]{:S(2)}, u32[]{:S(2)}) collective-permute-start(bf16[146,1,1024]{2,0,1:T(8,128)(2,1)} %get-tuple-element.116), channel_id=1, source_target_pairs={{0,3},{1,0},{2,1},{3,2},{4,7},{5,4},{6,5},{7,6},{8,11},{9,8},{10,9... | collective-permute-start | bytes 897032 | tf_op jit(solution)/shard_map/ppermute | solution.py:195
  881.0 27.1 %collective-permute-start.2 = (bf16[146,1,1024]{2,0,1:T(8,128)(2,1)}, bf16[146,1,1024]{2,0,1:T(8,128)(2,1)}, u32[]{:S(2)}, u32[]{:S(2)}) collective-permute-start(bf16[146,1,1024]{2,0,1:T(8,128)(2,1)} %collective-permute-done), channel_id=1, source_target_pairs={{0,1},{1,2},{2,3},{3,0},{4,5},{5,6},{6,7},{7,4},{8,9},{9,10},{10,1... | collective-permute-start | bytes 897032 | tf_op jit(solution)/shard_map/ppermute | solution.py:190
  898.0 21.9 %slice-start.2 = ((s8[5980160]{0:T(1024)(128)(4,1)}), s8[1785856]{0:T(1024)(128)(4,1)S(1)}, s32[]{:S(2)}) async-start(s8[5980160]{0:T(1024)(128)(4,1)} %bitcast.223), calls=%async_computation.22 | async-start | bytes 3571712
  903.7 23.5 %collective-permute-start.5 = (bf16[146,1,1024]{2,0,1:T(8,128)(2,1)}, bf16[146,1,1024]{2,0,1:T(8,128)(2,1)}, u32[]{:S(2)}, u32[]{:S(2)}) collective-permute-start(bf16[146,1,1024]{2,0,1:T(8,128)(2,1)} %collective-permute-done.3), channel_id=1, source_target_pairs={{0,1},{1,2},{2,3},{3,0},{4,5},{5,6},{6,7},{7,4},{8,9},{9,10},{10,1... | collective-permute-start | bytes 897032 | tf_op jit(solution)/shard_map/ppermute | solution.py:190
  915.3 4.5 slice-start.3
  915.3 4.6 copy-start.18
  932.9 4.7 slice-start.1
  943.7 4.8 copy-start.29
  956.7 223.1 %all-reduce.26.cloned.1.call-start = ((), (), s32[]{:S(2)}) async-start(), calls=%async_computation.17 | async-start | bytes 9568256
  968.8 265.2 %reduce-scatter.15.cloned.1.call-start = ((), (), s32[]{:S(2)}) async-start(), calls=%async_computation.15 | async-start | bytes 4718592 | tf_op jit(solution)/shard_map/reduce_scatter | solution.py:262
  977.1 312.4 %reduce-scatter.17.cloned.1.call-start = ((), (), s32[]{:S(2)}) async-start(), calls=%async_computation.16 | async-start | bytes 4718592 | tf_op jit(solution)/shard_map/reduce_scatter | solution.py:263
  977.4 4.6 copy-start.38
  977.4 4.6 copy-start.43
  986.1 4.5 copy-start.70
  986.1 4.8 copy-start.33
  986.2 343.0 %reduce-scatter.13.cloned.1.call-start = ((), (), s32[]{:S(2)}) async-start(), calls=%async_computation.14 | async-start | bytes 1179648 | tf_op jit(solution)/shard_map/reduce_scatter | solution.py:261
  993.8 189.6 %copy-start.5 = (bf16[146,1,1024]{2,0,1:T(8,128)(2,1)S(1)}, bf16[146,1,1024]{2,0,1:T(8,128)(2,1)}, u32[]{:S(2)}) copy-start(bf16[146,1,1024]{2,0,1:T(8,128)(2,1)} %copy-done.4) | copy-start | bytes 897028
  993.8 189.7 %copy-start.45 = (f32[8,1,128]{2,1,0:T(1,128)S(1)}, f32[8,1,128]{2,1,0:T(1,128)}, u32[]{:S(2)}) copy-start(f32[8,1,128]{2,1,0:T(1,128)} %copy-done.44) | copy-start | bytes 12292
  993.8 189.7 %copy-start.50 = (f32[146]{0:T(256)S(1)}, f32[146]{0:T(256)}, u32[]{:S(2)}) copy-start(f32[146]{0:T(256)} %copy-done.49) | copy-start | bytes 1756
  993.8 189.9 %copy-start.69 = (f32[146]{0:T(256)S(1)}, f32[146]{0:T(256)}, u32[]{:S(2)}) copy-start(f32[146]{0:T(256)} %copy-done.68) | copy-start | bytes 1756
  993.8 190.0 %copy-start.3 = (bf16[146,1,1024]{2,0,1:T(8,128)(2,1)S(1)}, bf16[146,1,1024]{2,0,1:T(8,128)(2,1)}, u32[]{:S(2)}) copy-start(bf16[146,1,1024]{2,0,1:T(8,128)(2,1)} %copy-done.2) | copy-start | bytes 897028
  993.8 190.0 %copy-start.48 = (f32[146]{0:T(256)S(1)}, f32[146]{0:T(256)}, u32[]{:S(2)}) copy-start(f32[146]{0:T(256)} %copy-done.47) | copy-start | bytes 1756
  993.8 190.0 %copy-start.54 = (f32[146]{0:T(256)S(1)}, f32[146]{0:T(256)}, u32[]{:S(2)}) copy-start(f32[146]{0:T(256)} %copy-done.53) | copy-start | bytes 1756
  1183.8 27.4 %copy-start.13 = (f32[146,1,1024]{2,0,1:T(8,128)S(1)}, f32[146,1,1024]{2,0,1:T(8,128)}, u32[]{:S(2)}) copy-start(f32[146,1,1024]{2,0,1:T(8,128)} %copy-done.12) | copy-start | bytes 1794052
  1183.8 27.4 %copy-start.63 = (f32[146]{0:T(256)S(1)}, f32[146]{0:T(256)}, u32[]{:S(2)}) copy-start(f32[146]{0:T(256)} %copy-done.62) | copy-start | bytes 1756
  (53 other events, 157.5 us)
Sparse Core Ops, SparseCore 0:
  32.2 51.3 all-gather.15
  85.5 24.4 all-gather.17
  112.2 51.0 all-gather.25
  192.8 173.2 all-reduce.29
  368.0 26.8 all-gather.21
  397.0 51.0 all-gather.27
  450.3 49.8 all-gather.19
  501.8 49.8 all-gather.29
  553.7 26.9 all-gather.23
  582.2 51.0 all-gather.31
  646.4 214.8 all-reduce.27
  956.8 45.9 reduce-scatter.10
  1005.4 174.4 all-reduce.25
  1183.6 50.3 reduce-scatter.14
  1238.1 51.3 reduce-scatter.16
  1293.1 35.9 reduce-scatter.12
